TPU v7x, 32 devices: a whole 2x2x4 slice. The times are simulated.
32 devices in a mesh: group: 2 (over y), expert: 16 (over z, x, core).
Axes of the slice: x: 2, y: 2, z: 4, core: 2. Of those that a mesh axis runs over, the one named last changes fastest.
Arguments:
- values: bfloat16 [128, 7168], P(('group', 'expert')), parts along dimension 0, may hold values from -6 to 6
- scales: float32 [128, 56], P(('group', 'expert')), parts along dimension 0, may hold values from 0.25 to 4
- routes: int32 [128, 8], P(('group', 'expert')), parts along dimension 0, may hold values from 0 to 15, all different within a row; in each aligned block of 4 rows (0 to 3, 4 to 7, ...) at most 3 rows name the same one
- weights: float32 [128, 8], P(('group', 'expert')), parts along dimension 0, may hold values from 0.1 to 1
- w_gate: bfloat16 [7168, 32768], P(None, 'expert'), may hold values from -0.0625 to 0.0625
- w_up: bfloat16 [7168, 32768], P(None, 'expert'), may hold values from -0.0625 to 0.0625
- w_down: bfloat16 [32768, 7168], P('expert'), may hold values from -0.125 to 0.125
Outputs:
- layer_out: bfloat16 [128, 7168], P(('group', 'expert')), parts along dimension 0
There are 2 independent parts, one for each index of `group`. A program takes and returns all parts, laid end to end along the dimension named above; an argument that names none is the same for every part. Nothing has to cross between parts.
Inputs may be any that keep to these rules, and one draw needn't show every extreme that they name: `routes`: each row names 8 different experts; among the 4 rows of one device at most 3 name the same expert, and in every draw some expert is named by exactly 3 rows of some device.
All inputs are finite; a program needn't handle non-finite values.
Results may differ from a plain program's by a relative error of at most 0.019.
Values may be sent and summed in bfloat16 or wider, within the bound.
A program may use at most 192 MiB of HBM per device.

v0:
```python
import functools
import jax
import jax.numpy as jnp
from jax import lax
from jax.experimental import pallas as pl
from jax.experimental.pallas import tpu as pltpu
from jax.sharding import PartitionSpec as P

BLOCK = 128
EXPERTS = 16
LANES = 128
MESH = pl.DeviceIdType.MESH
CHUNK = 1024


def kernel(
    outer, group_size, tok, width, ffh,
    values, scales, routes, weights, wg_hbm, wu_hbm, wd_hbm, out,
    zb, x, wg, wu, wd, accg, accu, hid, wcol, tmp, r1, r2a, r2b, r3a, r3b, zret,
    wsem, ssem, rsem,
):
    g = lax.axis_index("group")
    e = lax.axis_index("expert")
    zi, xi, ci = e // 4, (e // 2) % 2, e % 2
    rows = tok * outer
    total = 8 * rows
    nk = width // CHUNK
    cut = CHUNK * ((nk + 1) // 2)
    dispatch = [(0, cut, range(0, cut // CHUNK)), (cut, width + LANES, range(cut // CHUNK, nk))]
    mblk = min(total, 128)
    ntile = min(256, ffh)

    peer_x = (g, zi * 4 + (1 - xi) * 2 + ci)
    peer_y = (1 - g, e)
    peer_c = (g, zi * 4 + xi * 2 + (1 - ci))

    def peer_z(p):
        return (g, lax.rem(zi + p, outer) * 4 + xi * 2 + ci)

    def weight_copies(j):
        half = pl.ds(pl.multiple_of(g * ffh, ffh), ffh)
        part = pl.ds(j * CHUNK, CHUNK)
        return (
            pltpu.make_async_copy(wg_hbm.at[part, half], wg.at[j], wsem.at[0, j]),
            pltpu.make_async_copy(wu_hbm.at[part, half], wu.at[j], wsem.at[1, j]),
            pltpu.make_async_copy(wd_hbm.at[half, part], wd.at[j], wsem.at[2, j]),
        )

    copies = [weight_copies(j) for j in range(nk)]
    for j in range(nk):
        copies[j][0].start()
        copies[j][1].start()
    for j in range(nk):
        copies[j][2].start()

    barrier = pltpu.get_barrier_semaphore()
    for dev in [peer_x, peer_y, peer_c] + [peer_z(p) for p in range(1, outer)]:
        pl.semaphore_signal(barrier, inc=1, device_id=dev, device_id_type=MESH)

    for b in range(width // BLOCK):
        cols = slice(b * BLOCK, (b + 1) * BLOCK)
        row = values[:, cols].astype(jnp.float32) * scales[:, b : b + 1]
        zb[zi, :, cols] = row.astype(jnp.bfloat16)
    lane = lax.broadcasted_iota(jnp.int32, (tok, LANES), 1)
    rw = jnp.zeros((tok, LANES), jnp.float32)
    low_lane = jnp.where(lane < 64, lane, lane - 64)
    for k in range(routes.shape[1]):
        rw = rw + jnp.where(low_lane == routes[:, k : k + 1], weights[:, k : k + 1], 0.0)
    high = rw.astype(jnp.bfloat16).astype(jnp.float32)
    zb[zi, :, width:] = jnp.where(lane < 64, high, rw - high).astype(jnp.bfloat16)

    pl.semaphore_wait(barrier, 3 + outer - 1)

    count = [0]
    sent = []

    def move(src, dst, dev):
        n = count[0]
        count[0] += 1
        copy = pltpu.make_async_remote_copy(
            src_ref=src, dst_ref=dst, send_sem=ssem.at[n], recv_sem=rsem.at[n],
            device_id=dev, device_id_type=MESH,
        )
        sent.append(copy)
        return copy

    def landed(view, copy_index):
        pltpu.make_async_remote_copy(
            src_ref=view, dst_ref=view, send_sem=ssem.at[copy_index],
            recv_sem=rsem.at[copy_index], device_id=peer_c, device_id_type=MESH,
        ).wait_recv()

    def block(c, y, xx, c0, c1):
        start = pl.multiple_of((c * 4 + y * 2 + xx) * rows, 16)
        return x.at[pl.ds(start, rows), pl.ds(c0, c1 - c0)]

    def push(view, dev):
        copy = move(view, view, dev)
        copy.start()
        return count[0] - 1

    zid = []
    for c0, c1, _ in dispatch:
        ids = []
        for p in range(1, outer):
            ids.append(push(zb.at[zi, :, pl.ds(c0, c1 - c0)], peer_z(p)))
        zid.append(ids)
    second = []
    for d, (c0, c1, _) in enumerate(dispatch):
        for p in range(1, outer):
            source = lax.rem(zi - p + outer, outer)
            landed(zb.at[source, :, pl.ds(c0, c1 - c0)], zid[d][p - 1])
        for z in range(outer):
            tmp[z * tok : (z + 1) * tok, : c1 - c0] = zb[z, :, c0:c1].astype(jnp.float32)
        start = pl.multiple_of((ci * 4 + g * 2 + xi) * rows, 16)
        x[pl.ds(start, rows), c0:c1] = tmp[:, : c1 - c0].astype(jnp.bfloat16)
        mine = block(ci, g, xi, c0, c1)
        second.append((push(mine, peer_x), push(mine, peer_y), push(mine, peer_c)))
    third = []
    for d, (c0, c1, _) in enumerate(dispatch):
        mid = (c0 + c1) // 2 // 128 * 128
        landed(block(ci, g, 1 - xi, c0, c1), second[d][0])
        a = push(block(ci, g, 1 - xi, c0, mid), peer_y)
        ca = push(block(ci, g, 1 - xi, c0, c1), peer_c)
        landed(block(ci, 1 - g, xi, c0, c1), second[d][1])
        b = push(block(ci, 1 - g, xi, mid, c1), peer_x)
        cb = push(block(ci, 1 - g, xi, c0, c1), peer_c)
        third.append((a, b, ca, cb))
    fourth = []
    for d, (c0, c1, _) in enumerate(dispatch):
        mid = (c0 + c1) // 2 // 128 * 128
        landed(block(ci, 1 - g, 1 - xi, c0, mid), third[d][0])
        fa = push(block(ci, 1 - g, 1 - xi, c0, mid), peer_c)
        landed(block(ci, 1 - g, 1 - xi, mid, c1), third[d][1])
        fb = push(block(ci, 1 - g, 1 - xi, mid, c1), peer_c)
        fourth.append((fa, fb))

    accg[...] = jnp.zeros_like(accg)
    accu[...] = jnp.zeros_like(accu)
    for d, (c0, c1, chunks) in enumerate(dispatch):
        mid = (c0 + c1) // 2 // 128 * 128
        oc = 1 - ci
        landed(block(oc, g, xi, c0, c1), second[d][2])
        landed(block(oc, g, 1 - xi, c0, c1), third[d][2])
        landed(block(oc, 1 - g, xi, c0, c1), third[d][3])
        landed(block(oc, 1 - g, 1 - xi, c0, mid), fourth[d][0])
        landed(block(oc, 1 - g, 1 - xi, mid, c1), fourth[d][1])
        for j in chunks:
            copies[j][0].wait()
            copies[j][1].wait()

            @pl.loop(0, total // mblk)
            def _(m):
                at = pl.ds(pl.multiple_of(m * mblk, mblk), mblk)
                lhs = x[at, j * CHUNK : (j + 1) * CHUNK]

                @pl.loop(0, ffh // ntile)
                def _(n):
                    cols = pl.ds(pl.multiple_of(n * ntile, ntile), ntile)
                    accg[at, cols] += jnp.dot(
                        lhs, wg[j, :, cols], preferred_element_type=jnp.float32
                    )
                    accu[at, cols] += jnp.dot(
                        lhs, wu[j, :, cols], preferred_element_type=jnp.float32
                    )

    mine_e = e // group_size

    @pl.loop(0, total // mblk)
    def _(m):
        at = pl.ds(pl.multiple_of(m * mblk, mblk), mblk)
        gate = accg[at, :]
        hid[at, :] = (gate / (1.0 + jnp.exp(-gate)) * accu[at, :]).astype(jnp.bfloat16)
        wide = x[at, width:].astype(jnp.float32)
        lanes = lax.broadcasted_iota(jnp.int32, (mblk, LANES), 1)
        keep = (lanes == mine_e) | (lanes == mine_e + 64)
        column = jnp.sum(jnp.where(keep, wide, 0.0), axis=1, keepdims=True)
        wcol[at, :] = jnp.broadcast_to(column, (mblk, LANES))

    for copy in sent:
        copy.wait_send()
    sent.clear()

    own = pl.ds(pl.multiple_of(ci * 4 * rows, 16), 4 * rows)
    other = pl.ds(pl.multiple_of((1 - ci) * 4 * rows, 16), 4 * rows)
    half = CHUNK // 2
    ids = [dict() for _ in range(nk)]
    dtile = 256

    def stage_down(j):
        copies[j][2].wait()

        @pl.loop(0, total // mblk)
        def _(m):
            at = pl.ds(pl.multiple_of(m * mblk, mblk), mblk)

            @pl.loop(0, CHUNK // dtile)
            def _(n):
                cols = pl.ds(pl.multiple_of(n * dtile, dtile), dtile)
                to = pl.ds(pl.multiple_of(j * CHUNK + n * dtile, dtile), dtile)
                got = jnp.dot(hid[at, :], wd[j, :, cols], preferred_element_type=jnp.float32)
                x[at, to] = (got * wcol[at, 0:1]).astype(jnp.bfloat16)

        cols = pl.ds(j * CHUNK, CHUNK)
        move(x.at[other, cols], r1.at[:, cols], peer_c).start()
        ids[j]["c"] = count[0] - 1

    def stage_core(j):
        cols = pl.ds(j * CHUNK, CHUNK)
        landed(r1.at[:, cols], ids[j]["c"])
        both = x[own, cols].astype(jnp.float32) + r1[:, cols].astype(jnp.float32)
        r1[:, cols] = both.astype(jnp.bfloat16)
        a, b = pl.ds(j * CHUNK, half), pl.ds(j * CHUNK + half, half)
        h = pl.ds(j * half, half)
        for y in range(2):
            start = pl.multiple_of((y * 2 + 1 - xi) * rows, 16)
            move(r1.at[pl.ds(start, rows), a], r2a.at[y, :, h], peer_x).start()
            ids[j]["x%d" % y] = count[0] - 1
        start = pl.multiple_of((1 - g) * 2 * rows, 16)
        move(r1.at[pl.ds(start, 2 * rows), b], r2b.at[:, h], peer_y).start()
        ids[j]["y"] = count[0] - 1

    def stage_plane(j):
        a, b = pl.ds(j * CHUNK, half), pl.ds(j * CHUNK + half, half)
        h = pl.ds(j * half, half)
        for y in range(2):
            landed(r2a.at[y, :, h], ids[j]["x%d" % y])
            start = pl.multiple_of((y * 2 + xi) * rows, 16)
            both = r1[pl.ds(start, rows), a].astype(jnp.float32) + r2a[y, :, h].astype(jnp.float32)
            r2a[y, :, h] = both.astype(jnp.bfloat16)
        move(r2a.at[1 - g, :, h], r3a.at[:, h], peer_y).start()
        ids[j]["a"] = count[0] - 1
        landed(r2b.at[:, h], ids[j]["y"])
        start = pl.multiple_of(g * 2 * rows, 16)
        both = r1[pl.ds(start, 2 * rows), b].astype(jnp.float32) + r2b[:, h].astype(jnp.float32)
        r2b[:, h] = both.astype(jnp.bfloat16)
        start = pl.multiple_of((1 - xi) * rows, 16)
        move(r2b.at[pl.ds(start, rows), h], r3b.at[:, h], peer_x).start()
        ids[j]["b"] = count[0] - 1

    def stage_line(j):
        h = pl.ds(j * half, half)
        landed(r3a.at[:, h], ids[j]["a"])
        tmp[:, 0:half] = r2a[g, :, h].astype(jnp.float32) + r3a[:, h].astype(jnp.float32)
        landed(r3b.at[:, h], ids[j]["b"])
        start = pl.multiple_of(xi * rows, 16)
        tmp[:, half:CHUNK] = (
            r2b[pl.ds(start, rows), h].astype(jnp.float32) + r3b[:, h].astype(jnp.float32)
        )
        cols = pl.ds(j * CHUNK, CHUNK)
        for z in range(outer):
            zb[z, :, cols] = tmp[z * tok : (z + 1) * tok, 0:CHUNK].astype(jnp.bfloat16)
        ids[j]["z"] = []
        for p in range(1, outer):
            to = lax.rem(zi + p, outer)
            move(zb.at[to, :, cols], zret.at[zi, :, cols], peer_z(p)).start()
            ids[j]["z"].append(count[0] - 1)

    def stage_out(j):
        cols = pl.ds(j * CHUNK, CHUNK)
        sums = zb[zi, :, cols].astype(jnp.float32)
        for p in range(1, outer):
            source = lax.rem(zi - p + outer, outer)
            landed(zret.at[source, :, cols], ids[j]["z"][p - 1])
            sums = sums + zret[source, :, cols].astype(jnp.float32)
        out[:, cols] = sums.astype(jnp.bfloat16)

    stages = (stage_down, stage_core, stage_plane, stage_line, stage_out)
    for step in range(nk + len(stages) - 1):
        for s, stage in enumerate(stages):
            if 0 <= step - s < nk:
                stage(step - s)
    for copy in sent:
        copy.wait_send()


def body(values, scales, routes, weights, w_gate, w_up, w_down):
    devices = lax.axis_size("expert")
    outer = devices // 4
    tok, width = values.shape
    ffh = w_gate.shape[1] // 2
    rows = tok * outer
    nk = width // CHUNK
    bf, f32 = jnp.bfloat16, jnp.float32
    n_copies = 2 * (outer - 1 + 9) + nk * (6 + outer - 1)
    vmem = pl.BlockSpec(memory_space=pltpu.VMEM)
    hbm = pl.BlockSpec(memory_space=pl.ANY)
    macs = 8 * rows * width * ffh * 3
    return pl.pallas_call(
        functools.partial(kernel, outer, devices // EXPERTS, tok, width, ffh),
        out_shape=jax.ShapeDtypeStruct((tok, width), bf),
        in_specs=[vmem] * 4 + [hbm] * 3,
        out_specs=vmem,
        scratch_shapes=[
            pltpu.VMEM((outer, tok, width + LANES), bf),
            pltpu.VMEM((8 * rows, width + LANES), bf),
            pltpu.VMEM((nk, CHUNK, ffh), bf),
            pltpu.VMEM((nk, CHUNK, ffh), bf),
            pltpu.VMEM((nk, ffh, CHUNK), bf),
            pltpu.VMEM((8 * rows, ffh), f32),
            pltpu.VMEM((8 * rows, ffh), f32),
            pltpu.VMEM((8 * rows, ffh), bf),
            pltpu.VMEM((8 * rows, LANES), f32),
            pltpu.VMEM((rows, CHUNK * ((nk + 1) // 2)), f32),
            pltpu.VMEM((4 * rows, width), bf),
            pltpu.VMEM((2, rows, width // 2), bf),
            pltpu.VMEM((2 * rows, width // 2), bf),
            pltpu.VMEM((rows, width // 2), bf),
            pltpu.VMEM((rows, width // 2), bf),
            pltpu.VMEM((outer, tok, width), bf),
            pltpu.SemaphoreType.DMA((3, nk)),
            pltpu.SemaphoreType.DMA((n_copies,)),
            pltpu.SemaphoreType.DMA((n_copies,)),
        ],
        compiler_params=pltpu.CompilerParams(
            collective_id=0, has_side_effects=True, vmem_limit_bytes=60 * 2**20
        ),
        cost_estimate=pl.CostEstimate(
            flops=2 * macs, bytes_accessed=6 * width * ffh, transcendentals=8 * rows * ffh
        ),
    )(values, scales, routes, weights, w_gate, w_up, w_down)


def solution(mesh):
    return jax.shard_map(
        body,
        mesh=mesh,
        in_specs=(
            P(("group", "expert"), None),
            P(("group", "expert"), None),
            P(("group", "expert"), None),
            P(("group", "expert"), None),
            P(None, "expert"),
            P(None, "expert"),
            P("expert", None),
        ),
        out_specs=P(("group", "expert"), None),
        check_vma=False,
    )
```

profile of v0, /device:TPU:0, one launch (start us, length us, event | category | flops | bytes accessed | tf_op | source)
XLA Modules:
  0.0 60.8 jit_solution(10733911902642191698)
XLA Ops:
  0.0 59.4 %shard_map.73 = bf16[4,7168]{1,0:T(4,128)(2,1)} custom-call(bf16[4,7168]{1,0:T(4,128)(2,1)} %values.1, f32[4,56]{1,0:T(4,128)} %scales.1, s32[4,8]{1,0:T(4,128)} %routes.1, f32[4,8]{1,0:T(4,128)} %weights.1, bf16[7168,2048]{1,0:T(8,128)(2,1)} %wg_hbm.1, bf16[7168,2048]{1,0:T(8,128)(2,1)} %wu_hbm.1, bf16[2048,7168]{1,0:T(8,128)(2,1)} %wd_hbm.1), custom_call_target="tpu_custom_call" | custom-call | flops 5637144576 | bytes 44040192 | tf_op jit(solution)/shard_map/pallas_call | solution.py:289
  59.4 1.5 %copy.9 = bf16[4,7168]{1,0:T(4,128)(2,1)} copy(bf16[4,7168]{1,0:T(4,128)(2,1)} %shard_map.73) | data formatting | bytes 114688
where the time goes:
time: 61 us; the launch traced here: 60.8 us
  Pallas kernels  59.4 us (97%)
  local copies, waits for them, and re-layouts  1.46 us (2%)
    pallas_call x1, Pallas kernels, body(): pl.pallas_call(functools.partial(kernel, outer, devices // EXPERTS, tok,...  59.4 us
    unnamed x1, local copies, waits for them, and re-layouts  1.46 us

commit v1 on v0

--- a/solution.py
+++ b/solution.py
@@ -11,6 +11,9 @@
 LANES = 128
 MESH = pl.DeviceIdType.MESH
 CHUNK = 1024
+GATHER_LAG = 3
+RETURN_LAG = 3
+TILE = 1024
 
 
 def kernel(
@@ -25,10 +28,9 @@
     rows = tok * outer
     total = 8 * rows
     nk = width // CHUNK
-    cut = CHUNK * ((nk + 1) // 2)
-    dispatch = [(0, cut, range(0, cut // CHUNK)), (cut, width + LANES, range(cut // CHUNK, nk))]
+    edges = [(j * CHUNK, (j + 1) * CHUNK + (LANES if j == nk - 1 else 0)) for j in range(nk)]
     mblk = min(total, 128)
-    ntile = min(256, ffh)
+    ntile = min(TILE, ffh)
 
     peer_x = (g, zi * 4 + (1 - xi) * 2 + ci)
     peer_y = (1 - g, e)
@@ -100,13 +102,15 @@
         return count[0] - 1
 
     zid = []
-    for c0, c1, _ in dispatch:
+    for c0, c1 in edges:
         ids = []
         for p in range(1, outer):
             ids.append(push(zb.at[zi, :, pl.ds(c0, c1 - c0)], peer_z(p)))
         zid.append(ids)
-    second = []
-    for d, (c0, c1, _) in enumerate(dispatch):
+    second, third, fourth = [], [], []
+
+    def gather_line(d):
+        c0, c1 = edges[d]
         for p in range(1, outer):
             source = lax.rem(zi - p + outer, outer)
             landed(zb.at[source, :, pl.ds(c0, c1 - c0)], zid[d][p - 1])
@@ -116,9 +120,10 @@
         x[pl.ds(start, rows), c0:c1] = tmp[:, : c1 - c0].astype(jnp.bfloat16)
         mine = block(ci, g, xi, c0, c1)
         second.append((push(mine, peer_x), push(mine, peer_y), push(mine, peer_c)))
-    third = []
-    for d, (c0, c1, _) in enumerate(dispatch):
-        mid = (c0 + c1) // 2 // 128 * 128
+
+    def gather_plane(d):
+        c0, c1 = edges[d]
+        mid = c0 + CHUNK // 2
         landed(block(ci, g, 1 - xi, c0, c1), second[d][0])
         a = push(block(ci, g, 1 - xi, c0, mid), peer_y)
         ca = push(block(ci, g, 1 - xi, c0, c1), peer_c)
@@ -126,43 +131,52 @@
         b = push(block(ci, 1 - g, xi, mid, c1), peer_x)
         cb = push(block(ci, 1 - g, xi, c0, c1), peer_c)
         third.append((a, b, ca, cb))
-    fourth = []
-    for d, (c0, c1, _) in enumerate(dispatch):
-        mid = (c0 + c1) // 2 // 128 * 128
+
+    def gather_corner(d):
+        c0, c1 = edges[d]
+        mid = c0 + CHUNK // 2
         landed(block(ci, 1 - g, 1 - xi, c0, mid), third[d][0])
         fa = push(block(ci, 1 - g, 1 - xi, c0, mid), peer_c)
         landed(block(ci, 1 - g, 1 - xi, mid, c1), third[d][1])
         fb = push(block(ci, 1 - g, 1 - xi, mid, c1), peer_c)
         fourth.append((fa, fb))
 
-    accg[...] = jnp.zeros_like(accg)
-    accu[...] = jnp.zeros_like(accu)
-    for d, (c0, c1, chunks) in enumerate(dispatch):
-        mid = (c0 + c1) // 2 // 128 * 128
+    def project(d):
+        c0, c1 = edges[d]
+        mid = c0 + CHUNK // 2
         oc = 1 - ci
         landed(block(oc, g, xi, c0, c1), second[d][2])
         landed(block(oc, g, 1 - xi, c0, c1), third[d][2])
         landed(block(oc, 1 - g, xi, c0, c1), third[d][3])
         landed(block(oc, 1 - g, 1 - xi, c0, mid), fourth[d][0])
         landed(block(oc, 1 - g, 1 - xi, mid, c1), fourth[d][1])
-        for j in chunks:
-            copies[j][0].wait()
-            copies[j][1].wait()
-
-            @pl.loop(0, total // mblk)
-            def _(m):
-                at = pl.ds(pl.multiple_of(m * mblk, mblk), mblk)
-                lhs = x[at, j * CHUNK : (j + 1) * CHUNK]
-
-                @pl.loop(0, ffh // ntile)
-                def _(n):
-                    cols = pl.ds(pl.multiple_of(n * ntile, ntile), ntile)
-                    accg[at, cols] += jnp.dot(
-                        lhs, wg[j, :, cols], preferred_element_type=jnp.float32
-                    )
-                    accu[at, cols] += jnp.dot(
-                        lhs, wu[j, :, cols], preferred_element_type=jnp.float32
-                    )
+        copies[d][0].wait()
+        copies[d][1].wait()
+
+        @pl.loop(0, total // mblk)
+        def _(m):
+            at = pl.ds(pl.multiple_of(m * mblk, mblk), mblk)
+            lhs = x[at, c0 : c0 + CHUNK]
+
+            @pl.loop(0, ffh // ntile)
+            def _(n):
+                cols = pl.ds(pl.multiple_of(n * ntile, ntile), ntile)
+                gate = jnp.dot(lhs, wg[d, :, cols], preferred_element_type=jnp.float32)
+                up = jnp.dot(lhs, wu[d, :, cols], preferred_element_type=jnp.float32)
+                if d == 0:
+                    accg[at, cols] = gate
+                    accu[at, cols] = up
+                else:
+                    accg[at, cols] += gate
+                    accu[at, cols] += up
+
+    def run(stages, lag):
+        for step in range(nk + (len(stages) - 1) * lag):
+            for s, stage in enumerate(stages):
+                if 0 <= step - s * lag < nk:
+                    stage(step - s * lag)
+
+    run((gather_line, gather_plane, gather_corner, project), GATHER_LAG)
 
     mine_e = e // group_size
 
@@ -185,7 +199,7 @@
     other = pl.ds(pl.multiple_of((1 - ci) * 4 * rows, 16), 4 * rows)
     half = CHUNK // 2
     ids = [dict() for _ in range(nk)]
-    dtile = 256
+    dtile = TILE
 
     def stage_down(j):
         copies[j][2].wait()
@@ -265,11 +279,7 @@
             sums = sums + zret[source, :, cols].astype(jnp.float32)
         out[:, cols] = sums.astype(jnp.bfloat16)
 
-    stages = (stage_down, stage_core, stage_plane, stage_line, stage_out)
-    for step in range(nk + len(stages) - 1):
-        for s, stage in enumerate(stages):
-            if 0 <= step - s < nk:
-                stage(step - s)
+    run((stage_down, stage_core, stage_plane, stage_line, stage_out), RETURN_LAG)
     for copy in sent:
         copy.wait_send()
 
@@ -282,7 +292,7 @@
     rows = tok * outer
     nk = width // CHUNK
     bf, f32 = jnp.bfloat16, jnp.float32
-    n_copies = 2 * (outer - 1 + 9) + nk * (6 + outer - 1)
+    n_copies = nk * (outer - 1 + 9) + nk * (6 + outer - 1)
     vmem = pl.BlockSpec(memory_space=pltpu.VMEM)
     hbm = pl.BlockSpec(memory_space=pl.ANY)
     macs = 8 * rows * width * ffh * 3
@@ -301,7 +311,7 @@
             pltpu.VMEM((8 * rows, ffh), f32),
             pltpu.VMEM((8 * rows, ffh), bf),
             pltpu.VMEM((8 * rows, LANES), f32),
-            pltpu.VMEM((rows, CHUNK * ((nk + 1) // 2)), f32),
+            pltpu.VMEM((rows, CHUNK + LANES), f32),
             pltpu.VMEM((4 * rows, width), bf),
             pltpu.VMEM((2, rows, width // 2), bf),
             pltpu.VMEM((2 * rows, width // 2), bf),

time: 61 us -> 45.8 us (0.75)
  Pallas kernels: 59.4 us -> 44.2 us
    pallas_call x1, Pallas kernels: 59.4 us -> 44.2 us  [body(): pl.pallas_call(functools.partial(kernel, outer, devices // EXPERTS, tok,...]
where the time goes in v1:
time: 45.8 us; the launch traced here: 45.6 us
  Pallas kernels  44.2 us (97%)
  local copies, waits for them, and re-layouts  1.46 us (3%)
    pallas_call x1, Pallas kernels, body(): pl.pallas_call(functools.partial(kernel, outer, devices // EXPERTS, tok,...  44.2 us
    unnamed x1, local copies, waits for them, and re-layouts  1.46 us

profile of v1, /device:TPU:0, one launch (start us, length us, event | category | flops | bytes accessed | tf_op | source)
XLA Modules:
  0.0 45.6 jit_solution(1704876349193556739)
XLA Ops:
  0.0 44.2 %shard_map.73 = bf16[4,7168]{1,0:T(4,128)(2,1)} custom-call(bf16[4,7168]{1,0:T(4,128)(2,1)} %values.1, f32[4,56]{1,0:T(4,128)} %scales.1, s32[4,8]{1,0:T(4,128)} %routes.1, f32[4,8]{1,0:T(4,128)} %weights.1, bf16[7168,2048]{1,0:T(8,128)(2,1)} %wg_hbm.1, bf16[7168,2048]{1,0:T(8,128)(2,1)} %wu_hbm.1, bf16[2048,7168]{1,0:T(8,128)(2,1)} %wd_hbm.1), custom_call_target="tpu_custom_call" | custom-call | flops 5637144576 | bytes 44040192 | tf_op jit(solution)/shard_map/pallas_call | solution.py:299
  44.2 1.5 %copy.9 = bf16[4,7168]{1,0:T(4,128)(2,1)} copy(bf16[4,7168]{1,0:T(4,128)(2,1)} %shard_map.73) | data formatting | bytes 114688

commit v2 on v1

--- a/solution.py
+++ b/solution.py
@@ -12,7 +12,7 @@
 MESH = pl.DeviceIdType.MESH
 CHUNK = 1024
 GATHER_LAG = 3
-RETURN_LAG = 3
+RETURN_LAG = 4
 TILE = 1024
 
 
@@ -59,10 +59,12 @@
     for dev in [peer_x, peer_y, peer_c] + [peer_z(p) for p in range(1, outer)]:
         pl.semaphore_signal(barrier, inc=1, device_id=dev, device_id_type=MESH)
 
-    for b in range(width // BLOCK):
-        cols = slice(b * BLOCK, (b + 1) * BLOCK)
-        row = values[:, cols].astype(jnp.float32) * scales[:, b : b + 1]
-        zb[zi, :, cols] = row.astype(jnp.bfloat16)
+    def scale(c0):
+        for b in range(c0 // BLOCK, (c0 + CHUNK) // BLOCK):
+            cols = slice(b * BLOCK, (b + 1) * BLOCK)
+            row = values[:, cols].astype(jnp.float32) * scales[:, b : b + 1]
+            zb[zi, :, cols] = row.astype(jnp.bfloat16)
+
     lane = lax.broadcasted_iota(jnp.int32, (tok, LANES), 1)
     rw = jnp.zeros((tok, LANES), jnp.float32)
     low_lane = jnp.where(lane < 64, lane, lane - 64)
@@ -104,6 +106,7 @@
     zid = []
     for c0, c1 in edges:
         ids = []
+        scale(c0)
         for p in range(1, outer):
             ids.append(push(zb.at[zi, :, pl.ds(c0, c1 - c0)], peer_z(p)))
         zid.append(ids)

time: 45.8 us -> 46 us (level)
  no operation moved by 1% of the time
where the time goes in v2:
time: 46 us; the launch traced here: 45.8 us
  Pallas kernels  44.4 us (97%)
  local copies, waits for them, and re-layouts  1.46 us (3%)
    pallas_call x1, Pallas kernels, body(): pl.pallas_call(functools.partial(kernel, outer, devices // EXPERTS, tok,...  44.4 us
    unnamed x1, local copies, waits for them, and re-layouts  1.46 us

profile of v2, /device:TPU:0, one launch (start us, length us, event | category | flops | bytes accessed | tf_op | source)
XLA Modules:
  0.0 45.8 jit_solution(8486926019776687417)
XLA Ops:
  0.0 44.4 %shard_map.73 = bf16[4,7168]{1,0:T(4,128)(2,1)} custom-call(bf16[4,7168]{1,0:T(4,128)(2,1)} %values.1, f32[4,56]{1,0:T(4,128)} %scales.1, s32[4,8]{1,0:T(4,128)} %routes.1, f32[4,8]{1,0:T(4,128)} %weights.1, bf16[7168,2048]{1,0:T(8,128)(2,1)} %wg_hbm.1, bf16[7168,2048]{1,0:T(8,128)(2,1)} %wu_hbm.1, bf16[2048,7168]{1,0:T(8,128)(2,1)} %wd_hbm.1), custom_call_target="tpu_custom_call" | custom-call | flops 5637144576 | bytes 44040192 | tf_op jit(solution)/shard_map/pallas_call | solution.py:302
  44.4 1.5 %copy.9 = bf16[4,7168]{1,0:T(4,128)(2,1)} copy(bf16[4,7168]{1,0:T(4,128)(2,1)} %shard_map.73) | data formatting | bytes 114688
